TPU v7x, 32 devices: a whole 2x2x4 slice. The times are simulated.
32 devices in a mesh: groups: 2 (over y), loop: 4 (over z), enc: 2 (over x), rep: 2 (over core).
Axes of the slice: x: 2, y: 2, z: 4, core: 2. Of those that a mesh axis runs over, the one named last changes fastest.
Arguments:
- embeddings: bfloat16 [4096, 768], P(('groups', 'loop', 'rep'), 'enc'), parts along dimension 0, may hold values from -24 to 24
- head_weight: bfloat16 [768, 768], P('enc'), may hold values from -0.21875 to 0.21875
- gp_weights: float32 [4096], P('groups'), parts along dimension 0, may hold values from -24 to 24
- counts: int32 [8], P('groups'), parts along dimension 0, may hold values from 64 to 512, as said below
Outputs:
- embed_grad: bfloat16 [4096, 768], P(('groups', 'loop', 'rep'), 'enc'), parts along dimension 0
- head_grad: float32 [1536, 768], P(('groups', 'enc')), parts along dimension 0
There are 2 independent parts, one for each index of `groups`. A program takes and returns all parts, laid end to end along the dimension named above; an argument that names none is the same for every part. Nothing has to cross between parts.
Inputs may be any that keep to these rules, and one draw needn't show every extreme that they name: `counts`: some block is full and some block holds exactly 64 valid molecules.
All inputs are finite; a program needn't handle non-finite values.
Results may differ from a plain program's by a relative error of at most 0.019.
Values may be sent and summed in bfloat16 or wider, within the bound.
A program may use at most 64 MiB of HBM per device.

v0:
```python
import jax
import jax.numpy as jnp
from jax import lax
from jax.sharding import PartitionSpec as P

EPSILON = 1e-06


def passed_along(value, axis, steps):
    count = lax.axis_size(axis)
    pairs = [(source, (source + steps) % count) for source in range(count)]
    return lax.ppermute(value, axis, pairs)


def pass_forward(piece):
    return passed_along(piece, "loop", 1)


def body(embeddings, head_weight, gp_weights, counts):
    enc_size = lax.axis_size("enc")
    rep_size = lax.axis_size("rep")
    loop_size = lax.axis_size("loop")
    share_rows = embeddings.shape[0]
    piece_rows = share_rows // enc_size
    block_rows = share_rows * rep_size
    loop_index = lax.axis_index("loop")
    enc_index = lax.axis_index("enc")
    rep_index = lax.axis_index("rep")
    rows = embeddings
    own_feats = lax.psum_scatter(
        jnp.dot(rows, head_weight, preferred_element_type=jnp.float32),
        "enc",
        scatter_dimension=0,
        tiled=True,
    ).astype(jnp.bfloat16)
    block_feats = lax.all_gather(own_feats, ("enc", "rep"), axis=0, tiled=True)
    block_norms = jnp.sum(jnp.square(block_feats.astype(jnp.float32)), axis=1)
    offsets = (
        jnp.arange(rep_size, dtype=jnp.int32)[None, :, None] * share_rows
        + jnp.arange(enc_size, dtype=jnp.int32)[:, None, None] * piece_rows
        + jnp.arange(piece_rows, dtype=jnp.int32)[None, None, :]
    ).reshape(block_rows)
    own_base = lax.dynamic_slice_in_dim(gp_weights, loop_index * block_rows, block_rows)
    block_coef = (
        own_base.reshape(rep_size, enc_size, piece_rows).transpose(1, 0, 2).reshape(block_rows)
    )
    own_count = lax.dynamic_index_in_dim(counts, loop_index, keepdims=False)
    block_coef = jnp.where(offsets < own_count, block_coef, 0.0)
    piece_start = rep_index * share_rows + enc_index * piece_rows
    piece_offsets = piece_start + jnp.arange(piece_rows, dtype=jnp.int32)

    def tile(state, piece, anchor):
        anchor_count = lax.dynamic_index_in_dim(counts, anchor, keepdims=False)
        accum, quotient_sum = state
        piece_coef = lax.dynamic_slice_in_dim(
            gp_weights, anchor * block_rows + piece_start, piece_rows
        )
        piece_coef = jnp.where(piece_offsets < anchor_count, piece_coef, 0.0)
        piece_norms = jnp.sum(jnp.square(piece.astype(jnp.float32)), axis=1)
        scores = lax.dot_general(
            piece, block_feats, (((1,), (1,)), ((), ())), preferred_element_type=jnp.float32
        )
        denom = piece_norms[:, None] + block_norms[None, :] - scores + EPSILON
        inverse = 1.0 / (denom * denom)
        pair_coef = piece_coef[:, None] * block_coef[None, :]
        pair_weight = (pair_coef * (piece_norms[:, None] + block_norms[None, :]) * inverse).astype(
            jnp.bfloat16
        )
        quotient_sum = quotient_sum + jnp.sum(pair_coef * 2.0 * scores * inverse, axis=0)
        accum = accum + lax.dot_general(
            pair_weight, piece, (((0,), (0,)), ((), ())), preferred_element_type=jnp.float32
        )
        return (accum, quotient_sum)

    start_state = (
        jnp.zeros((block_rows, block_feats.shape[1]), jnp.float32),
        jnp.zeros((block_rows,), jnp.float32),
    )
    state = tile(start_state, own_feats, loop_index)

    def forward_step(step_index, carry):
        moving, inner = carry
        moving = pass_forward(moving)
        inner = tile(inner, moving, (loop_index - step_index - 1 + loop_size) % loop_size)
        return (moving, inner)

    moving, state = lax.fori_loop(0, loop_size - 1, forward_step, (own_feats, state))
    accum, quotient_sum = state
    grad_block = accum - block_feats.astype(jnp.float32) * quotient_sum[:, None]
    own_grad = lax.psum_scatter(
        grad_block.astype(jnp.bfloat16), ("enc", "rep"), scatter_dimension=0, tiled=True
    )
    piece = lax.all_gather(own_grad, "enc", axis=0, tiled=True)
    back = lax.dot_general(
        piece, head_weight, (((1,), (1,)), ((), ())), preferred_element_type=jnp.float32
    )
    embed_part = back
    rows = embeddings
    head_part = lax.dot_general(
        rows, piece, (((0,), (0,)), ((), ())), preferred_element_type=jnp.float32
    )
    embed_part, head_part = (embed_part, head_part)
    head_grad = lax.psum(head_part, ("loop", "rep"))
    return (embed_part.astype(jnp.bfloat16), head_grad)


def solution(mesh):
    placed = (P(("groups", "loop", "rep"), "enc"), P("enc", None), P("groups"), P("groups"))
    return jax.shard_map(
        body,
        mesh=mesh,
        in_specs=placed,
        out_specs=(P(("groups", "loop", "rep"), "enc"), P(("groups", "enc"), None)),
        check_vma=False,
    )
```

profile of v0, /device:TPU:1, one launch (start us, length us, event | category | flops | bytes accessed | tf_op | source)
XLA Modules:
  0.0 167.4 jit_solution(11172648524668776611)
XLA Ops:
  7.2 1.0 copy-done
  8.2 2.2 %fusion.40 = f32[256,768]{1,0:T(8,128)} fusion(bf16[256,384]{1,0:T(8,128)(2,1)} %param.6, bf16[384,768]{1,0:T(8,128)(2,1)S(1)} %copy-done), kind=kOutput, calls=%fused_computation.56 | convolution fusion | flops 150994944 | bytes 1572864 | tf_op jit(solution)/shard_map/dot_general | solution.py:31
  10.5 0.7 dynamic_slice.37
  11.2 0.8 dynamic_slice.39
  12.0 0.8 compare_select_fusion.1
  12.8 1.5 compare_select_fusion.2
  14.2 16.2 %reduce-scatter.3.cloned.1.call-done = f32[128,768]{1,0:T(8,128)} async-done(((f32[256,768]{1,0:T(8,128)}), f32[128,768]{1,0:T(8,128)}) %reduce-scatter.3.cloned.1.call-update) | async-done | bytes 393232 | tf_op jit(solution)/shard_map/reduce_scatter | solution.py:30
  30.4 1.1 multiply_reduce_fusion.1
  31.5 8.7 %all_gather.6 = bf16[512,768]{1,0:T(8,128)(2,1)S(1)} all-gather(bf16[128,768]{1,0:T(8,128)(2,1)S(1)} %get-tuple-element.541), channel_id=1, replica_groups=mesh['groups'=2,'loop'=4,'enc'=2,'rep'=2] {'enc','rep'}, dimensions={0}, use_global_device_ids=true | all-gather | bytes 983040 | tf_op jit(solution)/shard_map/all_gather | solution.py:36
  40.9 0.5 fusion.30
  41.4 25.5 %while.23 = (s32[]{:T(128)}, bf16[128,768]{1,0:T(8,128)(2,1)S(1)}, f32[512,768]{1,0:T(8,128)S(1)}, f32[512]{0:T(512)S(1)}, s32[]{:T(128)}, /*index=5*/s32[4]{0:T...) while((s32[]{:T(128)}, bf16[128,768]{1,0:T(8,128)(2,1)S(1)}, ...), condition=%wide.region_7.8_spmd.clone.clone, body=%wide.region_4.7_spmd.clone.clone.sunk | while | flops 203260192 | bytes 6246334 | solution.py:87
  41.4 1.3 collective-permute-start
  42.7 0.6 dynamic_slice.49
  43.3 1.4 compare_select_fusion.4
  44.7 5.0 %collective-permute-done = bf16[128,768]{1,0:T(8,128)(2,1)S(1)} collective-permute-done((bf16[128,768]{1,0:T(8,128)(2,1)S(1)}, bf16[128,768]{1,0:T(8,128)(2,1)S(1)}, u32[]{:S(2)}, u32[]{:S(2)}) %collective-permute-start) | collective-permute-done | bytes 196640 | tf_op jit(solution)/shard_map/while/body/eval_jaxpr/ppermute | solution.py:12
  50.2 0.6 convolution_add_fusion.2
  50.9 0.6 dynamic_slice.49
  51.5 1.4 compare_select_fusion.4
  52.9 5.2 %collective-permute-done = bf16[128,768]{1,0:T(8,128)(2,1)S(1)} collective-permute-done((bf16[128,768]{1,0:T(8,128)(2,1)S(1)}, bf16[128,768]{1,0:T(8,128)(2,1)S(1)}, u32[]{:S(2)}, u32[]{:S(2)}) %collective-permute-start) | collective-permute-done | bytes 196640 | tf_op jit(solution)/shard_map/while/body/eval_jaxpr/ppermute | solution.py:12
  58.2 0.4 fusion.62
  58.7 0.6 convolution_add_fusion.2
  59.4 0.6 dynamic_slice.49
  60.0 1.4 compare_select_fusion.4
  61.4 4.3 %collective-permute-done = bf16[128,768]{1,0:T(8,128)(2,1)S(1)} collective-permute-done((bf16[128,768]{1,0:T(8,128)(2,1)S(1)}, bf16[128,768]{1,0:T(8,128)(2,1)S(1)}, u32[]{:S(2)}, u32[]{:S(2)}) %collective-permute-start) | collective-permute-done | bytes 196640 | tf_op jit(solution)/shard_map/while/body/eval_jaxpr/ppermute | solution.py:12
  66.3 0.6 convolution_add_fusion.2
  66.9 1.1 fusion.21
  68.1 23.3 %reduce-scatter.5.cloned.1.call-done = bf16[128,768]{1,0:T(8,128)(2,1)} async-done(((bf16[512,768]{1,0:T(8,128)(2,1)}), bf16[128,768]{1,0:T(8,128)(2,1)}) %reduce-scatter.5.cloned.1.call-update) | async-done | bytes 196624 | tf_op jit(solution)/shard_map/reduce_scatter | solution.py:90
  91.4 6.6 %all_gather.7 = bf16[256,768]{1,0:T(8,128)(2,1)S(1)} all-gather(bf16[128,768]{1,0:T(8,128)(2,1)} %reduce-scatter.5.cloned.1.call-done), channel_id=1, replica_groups=mesh['groups'=2,'loop'=4,'enc'=2,'rep'=2] {'enc'}, dimensions={0}, use_global_device_ids=true | all-gather | bytes 589824 | tf_op jit(solution)/shard_map/all_gather | solution.py:93
  98.0 1.4 convolution_bitcast_fusion
  99.4 1.1 convolution_convert_fusion
  100.5 57.7 %all-reduce.2.cloned.1.call-done = f32[384,768]{0,1:T(8,128)} async-done(((f32[384,768]{0,1:T(8,128)}), f32[384,768]{0,1:T(8,128)}) %all-reduce.2.cloned.1.call-update) | async-done | bytes 1179664 | tf_op jit(solution)/shard_map/psum | solution.py:103
  158.2 2.7 %copy.9 = f32[384,768]{1,0:T(8,128)} copy(f32[384,768]{0,1:T(8,128)} %all-reduce.2.cloned.1.call-done) | data formatting | bytes 2359296
  (29 shorter events, 2.4 us)
Async XLA Ops:
  7.2 1.1 copy-start
  7.2 3.3 %copy-start.2 = (s32[4]{0:T(128)S(1)}, s32[4]{0:T(128)}, u32[]{:S(2)}) copy-start(s32[4]{0:T(128)} %param.9) | copy-start | bytes 52
  7.2 23.2 %reduce-scatter.3.cloned.1.call-start = ((), (), s32[]{:S(2)}) async-start(), calls=%async_computation.2 | async-start | bytes 1179648 | tf_op jit(solution)/shard_map/reduce_scatter | solution.py:30
  10.4 80.9 %reduce-scatter.5.cloned.1.call-start = ((), (), s32[]{:S(2)}) async-start(), calls=%async_computation.3 | async-start | bytes 983040 | tf_op jit(solution)/shard_map/reduce_scatter | solution.py:90
  41.4 8.2 %collective-permute-start = (bf16[128,768]{1,0:T(8,128)(2,1)S(1)}, bf16[128,768]{1,0:T(8,128)(2,1)S(1)}, u32[]{:S(2)}, u32[]{:S(2)}) collective-permute-start(bf16[128,768]{1,0:T(8,128)(2,1)S(1)} %get-tuple-element.558), channel_id=1, source_target_pairs={{0,4},{4,8},{8,12},{12,0},{1,5},{5,9},{9,13},{13,1},{2,6},{6,10},{... | collective-permute-start | bytes 589832 | tf_op jit(solution)/shard_map/while/body/eval_jaxpr/ppermute | solution.py:12
  50.8 7.3 %collective-permute-start = (bf16[128,768]{1,0:T(8,128)(2,1)S(1)}, bf16[128,768]{1,0:T(8,128)(2,1)S(1)}, u32[]{:S(2)}, u32[]{:S(2)}) collective-permute-start(bf16[128,768]{1,0:T(8,128)(2,1)S(1)} %get-tuple-element.558), channel_id=1, source_target_pairs={{0,4},{4,8},{8,12},{12,0},{1,5},{5,9},{9,13},{13,1},{2,6},{6,10},{... | collective-permute-start | bytes 589832 | tf_op jit(solution)/shard_map/while/body/eval_jaxpr/ppermute | solution.py:12
  59.3 6.4 %collective-permute-start = (bf16[128,768]{1,0:T(8,128)(2,1)S(1)}, bf16[128,768]{1,0:T(8,128)(2,1)S(1)}, u32[]{:S(2)}, u32[]{:S(2)}) collective-permute-start(bf16[128,768]{1,0:T(8,128)(2,1)S(1)} %get-tuple-element.558), channel_id=1, source_target_pairs={{0,4},{4,8},{8,12},{12,0},{1,5},{5,9},{9,13},{13,1},{2,6},{6,10},{... | collective-permute-start | bytes 589832 | tf_op jit(solution)/shard_map/while/body/eval_jaxpr/ppermute | solution.py:12
  66.9 31.1 %copy-start.1 = (bf16[256,384]{1,0:T(8,128)(2,1)S(1)}, bf16[256,384]{1,0:T(8,128)(2,1)}, u32[]{:S(2)}) copy-start(bf16[256,384]{1,0:T(8,128)(2,1)} %param.6) | copy-start | bytes 589828
  68.0 90.2 %all-reduce.2.cloned.1.call-start = ((), (), s32[]{:S(2)}) async-start(), calls=%async_computation.4 | async-start | bytes 2359296 | tf_op jit(solution)/shard_map/psum | solution.py:103
Sparse Core Ops, SparseCore 0:
  10.8 19.5 reduce-scatter.2
  68.1 23.1 reduce-scatter.4
  99.6 58.6 all-reduce.1
where the time goes:
time: 170 us; the launch traced here: 167 us
  waiting for transfers between devices  112 us (66%)
  blocking collectives  15.4 us (9%)
  between operations  13.8 us (8%)
  other arithmetic  9.37 us (6%)
  matrix products  8.65 us (5%)
  local copies, waits for them, and re-layouts  6.9 us (4%)
    psum x1, waiting for transfers between devices, body(): head_grad = lax.psum(head_part, ('loop', 'rep'))  57.7 us
    reduce_scatter x1, waiting for transfers between devices, body(): lax.psum_scatter(grad_block.astype(jnp.bfloat16), ('enc', 'rep'), scatter...  23.3 us
    reduce_scatter x1, waiting for transfers between devices, body(): lax.psum_scatter(jnp.dot(rows, head_weight, preferred_element_type=jnp.fl...  16.2 us
    ppermute x3, waiting for transfers between devices, passed_along(): return lax.ppermute(value, axis, pairs)  14.4 us
    all_gather x1, blocking collectives, body(): block_feats = lax.all_gather(own_feats, ('enc', 'rep'), axis=0, tiled=True)  8.72 us
    all_gather x1, blocking collectives, body(): piece = lax.all_gather(own_grad, 'enc', axis=0, tiled=True)  6.64 us
    select_n x4, other arithmetic, tile(): piece_coef = jnp.where(piece_offsets < anchor_count, piece_coef, 0.0)  5.68 us
    unnamed x7, local copies, waits for them, and re-layouts  3.67 us
  transfers between devices with their start and end apart: 6, of which 6 were waited for; matrix products, arithmetic and copies ran while one was open for 6% of the time, Pallas kernels for 0%

commit v1 on v0

v1 whole, which is shorter than its diff:
```python
import functools

import jax
import jax.numpy as jnp
from jax import lax
from jax.experimental import pallas as pl
from jax.experimental.pallas import tpu as pltpu
from jax.sharding import PartitionSpec as P

EPSILON = 1e-06
PARTS = 3
MESH_ID = pl.DeviceIdType.MESH


def kernel(
    sizes,
    emb_ref,
    head_ref,
    gp_ref,
    counts_ref,
    embed_out,
    head_out,
    e_all,
    w_all,
    f_own,
    n_own,
    accum,
    quot,
    h_own,
    h_core,
    h_recv,
    h_send,
    h_side,
    h_full,
    e_recv,
    z_send,
    zx_send,
    x_send,
    c_send,
    w_send,
    w_recv,
    wc_send,
    wc_recv,
    hc_send,
    hc_recv,
    hi_send,
    hi_recv,
    ho_send,
    hf_send,
    hf_recv,
):
    nz, nx, nc = sizes
    z = lax.axis_index("loop")
    x = lax.axis_index("enc")
    c = lax.axis_index("rep")
    other = 1 - c
    pair = z + 1 - 2 * lax.rem(z, 2)
    rows = emb_ref.shape[0]
    half, feats = w_all.shape[2], w_all.shape[3]
    width = feats // PARTS
    has_left = z > 0
    has_right = z < nz - 1

    def x_peer(j):
        return lax.rem(x + 1 + j, nx)

    def remote(src, dst, send, recv, device):
        return pltpu.make_async_remote_copy(
            src_ref=src, dst_ref=dst, send_sem=send, recv_sem=recv,
            device_id=device, device_id_type=MESH_ID,
        )

    def e_copy(b, cc, xx, send, device):
        slot = e_all.at[b, cc, xx]
        return remote(slot, slot, send, e_recv.at[b, cc, xx], device)

    def z_copy(b, d):
        return e_copy(b, c, x, z_send.at[d, b], {"loop": z + (1 if d == 0 else -1)})

    def zx_copy(j):
        return e_copy(z, c, x_peer(j), zx_send.at[j], {"loop": pair})

    def x_copy(b, j):
        return e_copy(b, c, x, x_send.at[j, b], {"enc": x_peer(j)})

    def c_copy(b, xx):
        return e_copy(b, c, xx, c_send.at[b, xx], {"rep": other})

    def e_wait(b, cc, xx):
        e_copy(b, cc, xx, c_send.at[b, xx], {"rep": other}).wait_recv()

    def w_copy(j):
        slot = w_all.at[x, c]
        return remote(slot, slot, w_send.at[j], w_recv.at[x], {"enc": x_peer(j)})

    def wc_copy(j):
        slot = w_all.at[x_peer(j), c]
        return remote(slot, slot, wc_send.at[j], wc_recv.at[j], {"rep": other})

    barrier = pltpu.get_barrier_semaphore()

    @pl.when(has_left)
    def _():
        pl.semaphore_signal(barrier, 1, device_id={"loop": z - 1}, device_id_type=MESH_ID)

    @pl.when(has_right)
    def _():
        pl.semaphore_signal(barrier, 1, device_id={"loop": z + 1}, device_id_type=MESH_ID)

    for j in range(nx - 1):
        pl.semaphore_signal(barrier, 1, device_id={"enc": x_peer(j)}, device_id_type=MESH_ID)
    pl.semaphore_signal(barrier, 1, device_id={"rep": other}, device_id_type=MESH_ID)

    e_all[z, c, x] = emb_ref[...]
    for cc in range(nc):
        w_all[x, cc] = head_ref[cc * half : (cc + 1) * half, :]
    accum[...] = jnp.zeros_like(accum)
    quot[...] = jnp.zeros_like(quot)

    pl.semaphore_wait(
        barrier, nx + has_left.astype(jnp.int32) + has_right.astype(jnp.int32)
    )

    def features(b, cc):
        total = jnp.dot(
            e_all[b, cc, 0], w_all[0].reshape(nc * half, feats),
            preferred_element_type=jnp.float32,
        )
        for xx in range(1, nx):
            total = total + jnp.dot(
                e_all[b, cc, xx], w_all[xx].reshape(nc * half, feats),
                preferred_element_type=jnp.float32,
            )
        total = total.astype(jnp.bfloat16)
        wide = total.astype(jnp.float32)
        return total, jnp.sum(wide * wide, axis=1, keepdims=True)

    def eye():
        return lax.broadcasted_iota(jnp.int32, (rows, rows), 0) == lax.broadcasted_iota(
            jnp.int32, (rows, rows), 1
        )

    def weight_row(b, cc):
        place = cc * rows + lax.broadcasted_iota(jnp.int32, (1, rows), 1)
        return jnp.where(place < counts_ref[b], gp_ref[pl.ds(b * nc + cc, 1), :], 0.0)

    def tile(b, cc, feat, norm):
        norm_row = jnp.sum(jnp.where(eye(), norm, 0.0), axis=0, keepdims=True)
        scores = lax.dot_general(
            f_own[...], feat, (((1,), (1,)), ((), ())), preferred_element_type=jnp.float32
        )
        both = n_own[...] + norm_row
        denom = both - scores + EPSILON
        scaled = weight_row(b, cc) * (1.0 / (denom * denom))
        quot[...] += jnp.sum(scaled * scores, axis=1, keepdims=True)
        accum[...] += jnp.dot(
            (both * scaled).astype(jnp.bfloat16), feat, preferred_element_type=jnp.float32
        )

    def stage_z(s, d):
        b = z - s if d == 0 else z + s
        valid = jnp.logical_and(b >= 0, b < nz)
        if d == 1:
            valid = jnp.logical_and(valid, s > 0)

        @pl.when(valid)
        def _():
            @pl.when(s > 0)
            def _():
                e_wait(b, c, x)

            @pl.when(jnp.logical_or(s == 0, has_right if d == 0 else has_left))
            def _():
                if d == 0:
                    @pl.when(has_right)
                    def _():
                        z_copy(b, 0).start()

                    @pl.when(jnp.logical_and(s == 0, has_left))
                    def _():
                        z_copy(b, 1).start()
                else:
                    z_copy(b, 1).start()

            @pl.when(b != pair)
            def _():
                for j in range(nx - 1):
                    x_copy(b, j).start()

            c_copy(b, x).start()

            @pl.when(s == 0)
            def _():
                for j in range(nx - 1):
                    w_copy(j).start()

    def stage_x(s, d):
        b = z - s if d == 0 else z + s
        valid = jnp.logical_and(jnp.logical_and(b >= 0, b < nz), s >= (1 if d else 0))

        @pl.when(valid)
        def _():
            for j in range(nx - 1):
                e_wait(b, c, x_peer(j))

                @pl.when(s == 0)
                def _():
                    zx_copy(j).start()

                c_copy(b, x_peer(j)).start()

    def stage_c(s, d):
        b = z - s if d == 0 else z + s
        valid = jnp.logical_and(jnp.logical_and(b >= 0, b < nz), s >= (1 if d else 0))

        @pl.when(valid)
        def _():
            @pl.when(s == 0)
            def _():
                for j in range(nx - 1):
                    peer = x_peer(j)
                    slot = w_all.at[peer, c]
                    remote(
                        slot, slot, w_send.at[j], w_recv.at[peer], {"enc": peer}
                    ).wait_recv()
                    wc_copy(j).start()
                for j in range(nx - 1):
                    slot = w_all.at[x_peer(j), other]
                    remote(
                        slot, slot, wc_send.at[j], wc_recv.at[j], {"rep": other}
                    ).wait_recv()
                feat, norm = features(z, c)
                f_own[...] = feat
                n_own[...] = norm

            for xx in range(nx):
                e_wait(b, other, xx)

            @pl.loop(0, nc)
            def _(cc):
                feat, norm = features(b, cc)
                tile(b, cc, feat, norm)

    @pl.loop(0, nz + 2)
    def _(t):
        @pl.when(t < nz)
        def _():
            stage_z(t, 0)
            stage_z(t, 1)

        @pl.when(jnp.logical_and(t >= 1, t < nz + 1))
        def _():
            stage_x(t - 1, 0)
            stage_x(t - 1, 1)

        @pl.when(t >= 2)
        def _():
            stage_c(t - 2, 0)
            stage_c(t - 2, 1)

    own_weight = jnp.sum(jnp.where(eye(), weight_row(z, c), 0.0), axis=1, keepdims=True)
    grad = (
        own_weight * (accum[...] - f_own[...].astype(jnp.float32) * (2.0 * quot[...]))
    ).astype(jnp.bfloat16)
    f_own[...] = grad

    middle = nz // 2
    left_side = z < middle
    inward = jnp.where(left_side, z + 1, z - 1)
    outward = jnp.where(left_side, z - 1, z + 1)
    is_middle = jnp.logical_or(z == middle - 1, z == middle)
    is_outer = jnp.logical_or(z == 0, z == nz - 1)
    spot = is_middle.astype(jnp.int32)

    def hc_copy(k):
        return remote(
            h_core.at[k], h_recv.at[k], hc_send.at[k], hc_recv.at[k], {"rep": other}
        )

    def hi_copy(k):
        return remote(
            h_send.at[k], h_side.at[spot, k], hi_send.at[k], hi_recv.at[spot, k],
            {"loop": inward},
        )

    def hi_wait(place, k):
        remote(
            h_send.at[k], h_side.at[place, k], hi_send.at[k], hi_recv.at[place, k],
            {"loop": inward},
        ).wait_recv()

    def ho_copy(k):
        slot = h_full.at[c, k]
        return remote(slot, slot, ho_send.at[k], hf_recv.at[c, k], {"loop": outward})

    def hf_copy(k):
        slot = h_full.at[c, k]
        return remote(slot, slot, hf_send.at[k], hf_recv.at[c, k], {"rep": other})

    for k in range(PARTS):
        part = lax.dot_general(
            emb_ref[...], f_own[:, k * width : (k + 1) * width], (((0,), (0,)), ((), ())),
            preferred_element_type=jnp.float32,
        )
        h_full_part = part.reshape(nc, half, width)

        @pl.when(c == 0)
        def _():
            h_own[k] = h_full_part[0]
            h_core[k] = h_full_part[1].astype(jnp.bfloat16)

        @pl.when(c == 1)
        def _():
            h_own[k] = h_full_part[1]
            h_core[k] = h_full_part[0].astype(jnp.bfloat16)

        hc_copy(k).start()

    for k in range(PARTS):
        hc_copy(k).wait_recv()
        h_own[k] = h_own[k] + h_recv[k].astype(jnp.float32)

        @pl.when(is_outer)
        def _():
            h_send[k] = h_own[k].astype(jnp.bfloat16)
            hi_copy(k).start()

    for k in range(PARTS):
        @pl.when(jnp.logical_not(is_outer))
        def _():
            hi_wait(0, k)
            h_send[k] = (h_own[k] + h_side[0, k].astype(jnp.float32)).astype(jnp.bfloat16)
            hi_copy(k).start()

    embed_out[...] = lax.dot_general(
        f_own[...], head_ref[...], (((1,), (1,)), ((), ())), preferred_element_type=jnp.float32
    ).astype(jnp.bfloat16)

    for k in range(PARTS):
        @pl.when(is_middle)
        def _():
            hi_wait(1, k)
            h_full[c, k] = (
                h_send[k].astype(jnp.float32) + h_side[1, k].astype(jnp.float32)
            ).astype(jnp.bfloat16)

        @pl.when(jnp.logical_not(is_middle))
        def _():
            ho_copy(k).wait_recv()

        @pl.when(jnp.logical_not(is_outer))
        def _():
            ho_copy(k).start()

        hf_copy(k).start()

    for k in range(PARTS):
        head_out[pl.ds(pl.multiple_of(c * half, half), half), k * width : (k + 1) * width] = (
            h_full[c, k].astype(jnp.float32)
        )

    for k in range(PARTS):
        slot = h_full.at[other, k]
        remote(slot, slot, hf_send.at[k], hf_recv.at[other, k], {"rep": other}).wait_recv()
        head_out[pl.ds(pl.multiple_of(other * half, half), half), k * width : (k + 1) * width] = (
            h_full[other, k].astype(jnp.float32)
        )

    @pl.loop(0, nz)
    def _(b):
        @pl.when(jnp.logical_and(b <= z, has_right))
        def _():
            z_copy(b, 0).wait_send()

        @pl.when(jnp.logical_and(b >= z, has_left))
        def _():
            z_copy(b, 1).wait_send()

        @pl.when(b != pair)
        def _():
            for j in range(nx - 1):
                x_copy(b, j).wait_send()

        for xx in range(nx):
            c_copy(b, xx).wait_send()

    for j in range(nx - 1):
        zx_copy(j).wait_send()
        w_copy(j).wait_send()
        wc_copy(j).wait_send()
    for k in range(PARTS):
        hc_copy(k).wait_send()
        hi_copy(k).wait_send()
        hf_copy(k).wait_send()

        @pl.when(jnp.logical_not(is_outer))
        def _():
            ho_copy(k).wait_send()


def body(embeddings, head_weight, gp_weights, counts):
    nz, nx, nc = (lax.axis_size(name) for name in ("loop", "enc", "rep"))
    rows, cols = embeddings.shape
    feats = head_weight.shape[1]
    half, width = cols // nc, feats // PARTS
    gp_rows = gp_weights.reshape(nz * nc, rows)
    vmem = pl.BlockSpec(memory_space=pltpu.VMEM)
    dma = pltpu.SemaphoreType.DMA
    return pl.pallas_call(
        functools.partial(kernel, (nz, nx, nc)),
        out_shape=(
            jax.ShapeDtypeStruct((rows, cols), jnp.bfloat16),
            jax.ShapeDtypeStruct((cols, feats), jnp.float32),
        ),
        in_specs=[vmem, vmem, vmem, pl.BlockSpec(memory_space=pltpu.SMEM)],
        out_specs=(vmem, vmem),
        scratch_shapes=[
            pltpu.VMEM((nz, nc, nx, rows, cols), jnp.bfloat16),
            pltpu.VMEM((nx, nc, half, feats), jnp.bfloat16),
            pltpu.VMEM((rows, feats), jnp.bfloat16),
            pltpu.VMEM((rows, 1), jnp.float32),
            pltpu.VMEM((rows, feats), jnp.float32),
            pltpu.VMEM((rows, 1), jnp.float32),
            pltpu.VMEM((PARTS, half, width), jnp.float32),
            pltpu.VMEM((PARTS, half, width), jnp.bfloat16),
            pltpu.VMEM((PARTS, half, width), jnp.bfloat16),
            pltpu.VMEM((PARTS, half, width), jnp.bfloat16),
            pltpu.VMEM((2, PARTS, half, width), jnp.bfloat16),
            pltpu.VMEM((nc, PARTS, half, width), jnp.bfloat16),
            dma((nz, nc, nx)),
            dma((2, nz)),
            dma((nx - 1,)),
            dma((nx - 1, nz)),
            dma((nz, nx)),
            dma((nx - 1,)),
            dma((nx,)),
            dma((nx - 1,)),
            dma((nx - 1,)),
            dma((PARTS,)),
            dma((PARTS,)),
            dma((PARTS,)),
            dma((2, PARTS)),
            dma((PARTS,)),
            dma((PARTS,)),
            dma((nc, PARTS)),
        ],
        compiler_params=pltpu.CompilerParams(
            collective_id=0, has_side_effects=True, vmem_limit_bytes=56 * 1024 * 1024
        ),
    )(embeddings, head_weight, gp_rows, counts)


def solution(mesh):
    placed = (P(("groups", "loop", "rep"), "enc"), P("enc", None), P("groups"), P("groups"))
    return jax.shard_map(
        body,
        mesh=mesh,
        in_specs=placed,
        out_specs=(P(("groups", "loop", "rep"), "enc"), P(("groups", "enc"), None)),
        check_vma=False,
    )
```

time: 170 us -> 62.4 us (0.37); the launches traced: 167 us -> 62.2 us
  waiting for transfers between devices: 112 us -> 0 us
  Pallas kernels: 0 us -> 56.3 us
  blocking collectives: 15.4 us -> 0 us
  between operations: 13.8 us -> 0.64 us
  other arithmetic: 9.37 us -> 0 us
  matrix products: 8.65 us -> 0 us
    psum x1 -> x0, waiting for transfers between devices: 57.7 us -> none  [body(): head_grad = lax.psum(head_part, ('loop', 'rep'))]
    pallas_call x0 -> x1, Pallas kernels: none -> 56.3 us  [body(): pl.pallas_call(functools.partial(kernel, (nz, nx, nc)), out_shape=(jax.Sh...]
    reduce_scatter x2 -> x0, waiting for transfers between devices: 39.5 us -> none  [the longest x1 23.3 us: body(): lax.psum_scatter(grad_block.astype(jnp.bfloat16), ('enc', 'rep'), scatter...]
    all_gather x2 -> x0, blocking collectives: 15.4 us -> none  [the longest x1 8.72 us: body(): block_feats = lax.all_gather(own_feats, ('enc', 'rep'), axis=0, tiled=True)]
    ppermute x3 -> x0, waiting for transfers between devices: 14.4 us -> none  [passed_along(): return lax.ppermute(value, axis, pairs)]
    dot_general x11 -> x0, matrix products: 8.65 us -> none  [the longest x4 2.22 us: tile(): lax.dot_general(pair_weight, piece, (((0,), (0,)), ((), ())), preferred_e...]
    select_n x5 -> x0, other arithmetic: 6.43 us -> none  [the longest x4 5.68 us: tile(): piece_coef = jnp.where(piece_offsets < anchor_count, piece_coef, 0.0)]
    dynamic_slice x5 -> x0, local copies, waits for them, and re-layouts: 3.19 us -> none  [the longest x4 2.43 us: tile(): anchor_count = lax.dynamic_index_in_dim(counts, anchor, keepdims=False)]
  transfers between devices with their start and end apart: 6 -> 0, of which waited for: 6 -> 0; matrix products, arithmetic and copies ran while one was open for 6% -> 0% of each run, Pallas kernels for 0% -> 0%
where the time goes in v1:
time: 62.4 us; the launch traced here: 62.2 us
  Pallas kernels  56.3 us (90%)
  local copies, waits for them, and re-layouts  5.28 us (8%)
  between operations  0.64 us (1%)
    pallas_call x1, Pallas kernels, body(): pl.pallas_call(functools.partial(kernel, (nz, nx, nc)), out_shape=(jax.Sh...  56.3 us
    unnamed x2, local copies, waits for them, and re-layouts  3.98 us
    reshape x1, local copies, waits for them, and re-layouts, body(): gp_rows = gp_weights.reshape(nz * nc, rows)  1.3 us

profile of v1, /device:TPU:1, one launch (start us, length us, event | category | flops | bytes accessed | tf_op | source)
XLA Modules:
  0.0 62.2 jit_solution(15243131535395913993)
XLA Ops:
  0.6 1.3 %reshape.7.gp_ref = f32[8,256]{1,0:T(8,128)} reshape(f32[2048]{0:T(1024)} %param.6) | data formatting | bytes 16384 | tf_op jit(solution)/shard_map/reshape | solution.py:406
  1.9 56.3 %shard_map.59 = (bf16[256,384]{1,0:T(8,128)(2,1)}, f32[384,768]{1,0:T(8,128)}) custom-call(bf16[256,384]{1,0:T(8,128)(2,1)} %emb_ref.1, bf16[384,768]{1,0:T(8,128)(2,1)} %head_ref.1, f32[8,256]{1,0:T(8,128)} %reshape.7.gp_ref, s32[4]{0:T(128)} %counts_ref.1), custom_call_target="tpu_custom_call" | custom-call | tf_op jit(solution)/shard_map/pallas_call | solution.py:409
  58.2 1.6 %copy.8 = bf16[256,384]{1,0:T(8,128)(2,1)} copy(bf16[256,384]{1,0:T(8,128)(2,1)} %get-tuple-element.4) | data formatting | bytes 393216
  59.8 2.4 %copy.9 = f32[384,768]{1,0:T(8,128)} copy(f32[384,768]{1,0:T(8,128)} %get-tuple-element.5) | data formatting | bytes 2359296

commit v2 on v1

v2 whole, which is shorter than its diff:
```python
import functools

import jax
import jax.numpy as jnp
from jax import lax
from jax.experimental import pallas as pl
from jax.experimental.pallas import tpu as pltpu
from jax.sharding import PartitionSpec as P

EPSILON = 1e-06
PARTS = 6
CHUNKS = 2
MESH_ID = pl.DeviceIdType.MESH


def kernel(
    sizes,
    emb_ref,
    head_ref,
    gp_ref,
    counts_ref,
    embed_out,
    head_out,
    e_all,
    w_all,
    f_own,
    n_own,
    accum,
    quot,
    h_own,
    h_core,
    h_recv,
    h_send,
    h_side,
    h_full,
    e_recv,
    z_send,
    x_send,
    c_send,
    w_send,
    w_recv,
    wy_send,
    wc_send,
    wc_recv,
    in_sem,
    hc_send,
    hc_recv,
    hi_send,
    hi_recv,
    ho_send,
    hf_send,
    hf_recv,
):
    nz, nx, nc, ng = sizes
    z = lax.axis_index("loop")
    x = lax.axis_index("enc")
    c = lax.axis_index("rep")
    g = lax.axis_index("groups")
    other = 1 - c
    rows, cols = e_all.shape[3:]
    piece = rows // CHUNKS
    quarter, feats = w_all.shape[3:]
    half = quarter * ng
    width = feats // PARTS
    has_left = z > 0
    has_right = z < nz - 1

    def x_peer(j):
        return lax.rem(x + 1 + j, nx)

    def remote(src, dst, send, recv, device):
        return pltpu.make_async_remote_copy(
            src_ref=src, dst_ref=dst, send_sem=send, recv_sem=recv,
            device_id=device, device_id_type=MESH_ID,
        )

    def g_peer(i):
        return lax.rem(g + 1 + i, ng)

    def e_copy(b, cc, xx, h, send, device):
        start = h * piece if isinstance(h, int) else pl.multiple_of(h * piece, piece)
        slot = e_all.at[b, cc, xx, pl.ds(start, piece)]
        return remote(slot, slot, send, e_recv.at[b, cc, xx, h], device)

    def z_copy(b, d, h):
        return e_copy(b, c, x, h, z_send.at[d, b, h], {"loop": z + (1 if d == 0 else -1)})

    def x_copy(b, j, h):
        return e_copy(b, c, x, h, x_send.at[j, b, h], {"enc": x_peer(j)})

    def c_copy(b, xx, h):
        return e_copy(b, c, xx, h, c_send.at[b, xx, h], {"rep": other})

    def e_wait(b, cc, xx, h):
        e_copy(b, cc, xx, h, c_send.at[b, xx, h], {"rep": other}).wait_recv()

    def w_copy(xx, gg, send, device):
        slot = w_all.at[xx, c, gg]
        return remote(slot, slot, send, w_recv.at[xx, gg], device)

    def wx_copy(j):
        return w_copy(x, g, w_send.at[j], {"enc": x_peer(j)})

    def wy_copy(j, i):
        return w_copy(x_peer(j), g, wy_send.at[j, i], {"groups": g_peer(i)})

    def w_wait(xx, gg):
        w_copy(xx, gg, w_send.at[0], {"rep": other}).wait_recv()

    def wc_copy(xx, cc, gg):
        slot = w_all.at[xx, cc, gg]
        return remote(slot, slot, wc_send.at[xx, gg], wc_recv.at[xx, gg], {"rep": other})

    own_emb = pltpu.make_async_copy(emb_ref, e_all.at[z, c, x], in_sem.at[0])
    own_emb.start()
    own_head = []
    for cc in range(nc):
        for gg in range(ng):
            start = (cc * ng + gg) * quarter
            own_head.append(
                pltpu.make_async_copy(
                    head_ref.at[pl.ds(start, quarter)],
                    w_all.at[x, cc, gg],
                    in_sem.at[1 + cc * ng + gg],
                )
            )
            own_head[-1].start()

    barrier = pltpu.get_barrier_semaphore()

    @pl.when(has_left)
    def _():
        pl.semaphore_signal(barrier, 1, device_id={"loop": z - 1}, device_id_type=MESH_ID)

    @pl.when(has_right)
    def _():
        pl.semaphore_signal(barrier, 1, device_id={"loop": z + 1}, device_id_type=MESH_ID)

    for j in range(nx - 1):
        pl.semaphore_signal(barrier, 1, device_id={"enc": x_peer(j)}, device_id_type=MESH_ID)
    pl.semaphore_signal(barrier, 1, device_id={"rep": other}, device_id_type=MESH_ID)

    for i in range(ng - 1):
        pl.semaphore_signal(barrier, 1, device_id={"groups": g_peer(i)}, device_id_type=MESH_ID)
    accum[...] = jnp.zeros_like(accum)
    quot[...] = jnp.zeros_like(quot)

    pl.semaphore_wait(
        barrier, nx + ng - 1 + has_left.astype(jnp.int32) + has_right.astype(jnp.int32)
    )
    own_emb.wait()
    for copy in own_head:
        copy.wait()
    for j in range(nx - 1):
        wx_copy(j).start()

    def features(b, cc):
        total = jnp.dot(
            e_all[b, cc, 0], w_all[0].reshape(cols, feats),
            preferred_element_type=jnp.float32,
        )
        for xx in range(1, nx):
            total = total + jnp.dot(
                e_all[b, cc, xx], w_all[xx].reshape(cols, feats),
                preferred_element_type=jnp.float32,
            )
        total = total.astype(jnp.bfloat16)
        wide = total.astype(jnp.float32)
        return total, jnp.sum(wide * wide, axis=1, keepdims=True)

    def eye():
        return lax.broadcasted_iota(jnp.int32, (rows, rows), 0) == lax.broadcasted_iota(
            jnp.int32, (rows, rows), 1
        )

    def weight_row(b, cc):
        place = cc * rows + lax.broadcasted_iota(jnp.int32, (1, rows), 1)
        lanes = gp_ref.shape[1]
        split = rows // lanes
        first = (b * nc + cc) * split
        held = [gp_ref[pl.ds(first + i, 1), :] for i in range(split)]
        return jnp.where(place < counts_ref[b], jnp.concatenate(held, axis=1), 0.0)

    def tile(b, cc, feat, norm):
        norm_row = jnp.sum(jnp.where(eye(), norm, 0.0), axis=0, keepdims=True)
        scores = lax.dot_general(
            f_own[...], feat, (((1,), (1,)), ((), ())), preferred_element_type=jnp.float32
        )
        both = n_own[...] + norm_row
        denom = both - scores + EPSILON
        scaled = weight_row(b, cc) * (1.0 / (denom * denom))
        quot[...] += jnp.sum(scaled * scores, axis=1, keepdims=True)
        accum[...] += jnp.dot(
            (both * scaled).astype(jnp.bfloat16), feat, preferred_element_type=jnp.float32
        )

    def at_step(s, d):
        b = z - s if d == 0 else z + s
        return b, jnp.logical_and(jnp.logical_and(b >= 0, b < nz), s >= (1 if d else 0))

    def stage_z(u, d):
        s, h = u // CHUNKS, lax.rem(u, CHUNKS)
        b, valid = at_step(s, d)

        @pl.when(valid)
        def _():
            @pl.when(s > 0)
            def _():
                e_wait(b, c, x, h)

            @pl.when(has_right if d == 0 else has_left)
            def _():
                z_copy(b, d, h).start()

            if d == 0:
                @pl.when(jnp.logical_and(s == 0, has_left))
                def _():
                    z_copy(b, 1, h).start()

            for j in range(nx - 1):
                x_copy(b, j, h).start()
            c_copy(b, x, h).start()

    def stage_x(u, d):
        s, h = u // CHUNKS, lax.rem(u, CHUNKS)
        b, valid = at_step(s, d)

        @pl.when(valid)
        def _():
            for j in range(nx - 1):
                e_wait(b, c, x_peer(j), h)
                c_copy(b, x_peer(j), h).start()

    def stage_w():
        for j in range(nx - 1):
            w_wait(x_peer(j), g)
            for i in range(ng - 1):
                wy_copy(j, i).start()
            wc_copy(x_peer(j), c, g).start()

    def stage_first():
        for j in range(nx - 1):
            for i in range(ng - 1):
                w_wait(x_peer(j), g_peer(i))
                wc_copy(x_peer(j), c, g_peer(i)).start()
        for j in range(nx - 1):
            for gg in range(ng):
                wc_copy(x_peer(j), other, gg).wait_recv()
        feat, norm = features(z, c)
        f_own[...] = feat
        n_own[...] = norm

    def stage_c(s, d):
        b, valid = at_step(s, d)

        @pl.when(valid)
        def _():
            for h in range(CHUNKS):
                for xx in range(nx):
                    e_wait(b, other, xx, h)

            @pl.loop(0, nc)
            def _(cc):
                feat, norm = features(b, cc)
                tile(b, cc, feat, norm)

    steps = nz * CHUNKS
    x_lag = 3
    c_lag = 3 + CHUNKS

    @pl.loop(0, steps + c_lag - 1)
    def _(t):
        @pl.when(t < steps)
        def _():
            stage_z(t, 0)
            stage_z(t, 1)

        @pl.when(t == 2)
        def _():
            stage_w()

        @pl.when(t == c_lag)
        def _():
            stage_first()

        @pl.when(jnp.logical_and(t >= c_lag, lax.rem(t - c_lag + CHUNKS, CHUNKS) == 0))
        def _():
            stage_c((t - c_lag) // CHUNKS, 0)
            stage_c((t - c_lag) // CHUNKS, 1)

        @pl.when(jnp.logical_and(t >= x_lag, t < steps + x_lag))
        def _():
            stage_x(t - x_lag, 0)
            stage_x(t - x_lag, 1)

    own_weight = jnp.sum(jnp.where(eye(), weight_row(z, c), 0.0), axis=1, keepdims=True)
    grad = (
        own_weight * (accum[...] - f_own[...].astype(jnp.float32) * (2.0 * quot[...]))
    ).astype(jnp.bfloat16)
    f_own[...] = grad

    middle = nz // 2
    left_side = z < middle
    inward = jnp.where(left_side, z + 1, z - 1)
    outward = jnp.where(left_side, z - 1, z + 1)
    is_middle = jnp.logical_or(z == middle - 1, z == middle)
    is_outer = jnp.logical_or(z == 0, z == nz - 1)
    spot = is_middle.astype(jnp.int32)

    def hc_copy(k):
        return remote(
            h_core.at[k], h_recv.at[k], hc_send.at[k], hc_recv.at[k], {"rep": other}
        )

    def hi_copy(k):
        return remote(
            h_send.at[k], h_side.at[spot, k], hi_send.at[k], hi_recv.at[spot, k],
            {"loop": inward},
        )

    def hi_wait(place, k):
        remote(
            h_send.at[k], h_side.at[place, k], hi_send.at[k], hi_recv.at[place, k],
            {"loop": inward},
        ).wait_recv()

    def ho_copy(k):
        slot = h_full.at[c, k]
        return remote(slot, slot, ho_send.at[k], hf_recv.at[c, k], {"loop": outward})

    def hf_copy(k):
        slot = h_full.at[c, k]
        return remote(slot, slot, hf_send.at[k], hf_recv.at[c, k], {"rep": other})

    for k in range(PARTS):
        part = lax.dot_general(
            e_all[z, c, x], f_own[:, k * width : (k + 1) * width], (((0,), (0,)), ((), ())),
            preferred_element_type=jnp.float32,
        )
        h_full_part = part.reshape(nc, half, width)

        @pl.when(c == 0)
        def _():
            h_own[k] = h_full_part[0]
            h_core[k] = h_full_part[1].astype(jnp.bfloat16)

        @pl.when(c == 1)
        def _():
            h_own[k] = h_full_part[1]
            h_core[k] = h_full_part[0].astype(jnp.bfloat16)

        hc_copy(k).start()

    for k in range(PARTS):
        hc_copy(k).wait_recv()
        h_own[k] = h_own[k] + h_recv[k].astype(jnp.float32)

        @pl.when(is_outer)
        def _():
            h_send[k] = h_own[k].astype(jnp.bfloat16)
            hi_copy(k).start()

    for k in range(PARTS):
        @pl.when(jnp.logical_not(is_outer))
        def _():
            hi_wait(0, k)
            h_send[k] = (h_own[k] + h_side[0, k].astype(jnp.float32)).astype(jnp.bfloat16)
            hi_copy(k).start()

    embed_out[...] = lax.dot_general(
        f_own[...], w_all[x].reshape(cols, feats), (((1,), (1,)), ((), ())), preferred_element_type=jnp.float32
    ).astype(jnp.bfloat16)

    for k in range(PARTS):
        @pl.when(is_middle)
        def _():
            hi_wait(1, k)
            h_full[c, k] = (
                h_send[k].astype(jnp.float32) + h_side[1, k].astype(jnp.float32)
            ).astype(jnp.bfloat16)

        @pl.when(jnp.logical_not(is_middle))
        def _():
            ho_copy(k).wait_recv()

        @pl.when(jnp.logical_not(is_outer))
        def _():
            ho_copy(k).start()

        hf_copy(k).start()

    for k in range(PARTS):
        slot = h_full.at[other, k]
        remote(slot, slot, hf_send.at[k], hf_recv.at[other, k], {"rep": other}).wait_recv()
    head_out[...] = h_full[...]

    @pl.loop(0, nz)
    def _(b):
        for h in range(CHUNKS):
            @pl.when(jnp.logical_and(b <= z, has_right))
            def _():
                z_copy(b, 0, h).wait_send()

            @pl.when(jnp.logical_and(b >= z, has_left))
            def _():
                z_copy(b, 1, h).wait_send()

            for j in range(nx - 1):
                x_copy(b, j, h).wait_send()
            for xx in range(nx):
                c_copy(b, xx, h).wait_send()

    for j in range(nx - 1):
        wx_copy(j).wait_send()
        for i in range(ng - 1):
            wy_copy(j, i).wait_send()
        for gg in range(ng):
            wc_copy(x_peer(j), c, gg).wait_send()
    for k in range(PARTS):
        hc_copy(k).wait_send()
        hi_copy(k).wait_send()
        hf_copy(k).wait_send()

        @pl.when(jnp.logical_not(is_outer))
        def _():
            ho_copy(k).wait_send()


def finish(embed_ref, head_ref, embed_out, head_out):
    cores, parts, half, width = head_ref.shape
    embed_out[...] = embed_ref[...]
    for cc in range(cores):
        for k in range(parts):
            head_out[cc * half : (cc + 1) * half, k * width : (k + 1) * width] = head_ref[
                cc, k
            ].astype(jnp.float32)


def body(embeddings, head_weight, gp_weights, counts):
    nz, nx, nc, ng = (lax.axis_size(name) for name in ("loop", "enc", "rep", "groups"))
    rows, cols = embeddings.shape
    feats = head_weight.shape[1]
    half, width = cols // nc, feats // PARTS
    if half % (16 * ng):
        raise ValueError("head rows")
    gp_rows = gp_weights.reshape(-1, 128)
    vmem = pl.BlockSpec(memory_space=pltpu.VMEM)
    hbm = pl.BlockSpec(memory_space=pl.ANY)
    dma = pltpu.SemaphoreType.DMA
    held = 2 * (nz * nc * nx * rows * cols + nx * cols * feats)
    embed_grad, head_sum = pl.pallas_call(
        functools.partial(kernel, (nz, nx, nc, ng)),
        out_shape=(
            jax.ShapeDtypeStruct((rows, cols), jnp.bfloat16),
            jax.ShapeDtypeStruct((nc, PARTS, half, width), jnp.bfloat16),
        ),
        in_specs=[hbm, hbm, vmem, pl.BlockSpec(memory_space=pltpu.SMEM)],
        out_specs=(vmem, vmem),
        scratch_shapes=[
            pltpu.VMEM((nz, nc, nx, rows, cols), jnp.bfloat16),
            pltpu.VMEM((nx, nc, ng, half // ng, feats), jnp.bfloat16),
            pltpu.VMEM((rows, feats), jnp.bfloat16),
            pltpu.VMEM((rows, 1), jnp.float32),
            pltpu.VMEM((rows, feats), jnp.float32),
            pltpu.VMEM((rows, 1), jnp.float32),
            pltpu.VMEM((PARTS, half, width), jnp.float32),
            pltpu.VMEM((PARTS, half, width), jnp.bfloat16),
            pltpu.VMEM((PARTS, half, width), jnp.bfloat16),
            pltpu.VMEM((PARTS, half, width), jnp.bfloat16),
            pltpu.VMEM((2, PARTS, half, width), jnp.bfloat16),
            pltpu.VMEM((nc, PARTS, half, width), jnp.bfloat16),
            dma((nz, nc, nx, CHUNKS)),
            dma((2, nz, CHUNKS)),
            dma((nx - 1, nz, CHUNKS)),
            dma((nz, nx, CHUNKS)),
            dma((nx - 1,)),
            dma((nx, ng)),
            dma((nx - 1, max(ng - 1, 1))),
            dma((nx, ng)),
            dma((nx, ng)),
            dma((1 + nc * ng,)),
            dma((PARTS,)),
            dma((PARTS,)),
            dma((PARTS,)),
            dma((2, PARTS)),
            dma((PARTS,)),
            dma((PARTS,)),
            dma((nc, PARTS)),
        ],
        compiler_params=pltpu.CompilerParams(
            collective_id=0, has_side_effects=True, vmem_limit_bytes=held + 20 * 1024 * 1024
        ),
    )(embeddings, head_weight, gp_rows, counts)
    return pl.pallas_call(
        finish,
        out_shape=(
            jax.ShapeDtypeStruct((rows, cols), jnp.bfloat16),
            jax.ShapeDtypeStruct((cols, feats), jnp.float32),
        ),
        in_specs=[vmem, vmem],
        out_specs=(vmem, vmem),
        compiler_params=pltpu.CompilerParams(vmem_limit_bytes=12 * 1024 * 1024),
    )(embed_grad, head_sum)


def solution(mesh):
    placed = (P(("groups", "loop", "rep"), "enc"), P("enc", None), P("groups"), P("groups"))
    return jax.shard_map(
        body,
        mesh=mesh,
        in_specs=placed,
        out_specs=(P(("groups", "loop", "rep"), "enc"), P(("groups", "enc"), None)),
        check_vma=False,
    )
```

time: 62.4 us -> 56.7 us (0.909)
  Pallas kernels: 56.3 us -> 52.5 us
  local copies, waits for them, and re-layouts: 5.28 us -> 3.33 us
    pallas_call x1 -> x2, Pallas kernels: 56.3 us -> 52.5 us  [the longest x1 51.3 us: body(): pl.pallas_call(functools.partial(kernel, (nz, nx, nc, ng)), out_shape=(ja...]
    reshape x1 -> x0, local copies, waits for them, and re-layouts: 1.3 us -> none  [body(): gp_rows = gp_weights.reshape(nz * nc, rows)]
    unnamed x2 -> x8, local copies, waits for them, and re-layouts: 3.98 us -> 3.33 us
where the time goes in v2:
time: 56.7 us; the launch traced here: 56.5 us
  Pallas kernels  52.5 us (93%)
  local copies, waits for them, and re-layouts  3.33 us (6%)
  between operations  0.65 us (1%)
    pallas_call x1, Pallas kernels, body(): pl.pallas_call(functools.partial(kernel, (nz, nx, nc, ng)), out_shape=(ja...  51.3 us
    unnamed x8, local copies, waits for them, and re-layouts  3.33 us
    pallas_call x1, Pallas kernels, body(): pl.pallas_call(finish, out_shape=(jax.ShapeDtypeStruct((rows, cols), jnp....  1.15 us

profile of v2, /device:TPU:1, one launch (start us, length us, event | category | flops | bytes accessed | tf_op | source)
XLA Modules:
  0.0 56.5 jit_solution(13554583603261154958)
XLA Ops:
  0.6 0.0 copy-start
  0.6 1.1 %copy-done = bf16[384,768]{1,0:T(8,128)(2,1)S(1)} copy-done((bf16[384,768]{1,0:T(8,128)(2,1)S(1)}, bf16[384,768]{1,0:T(8,128)(2,1)}, u32[]{:S(2)}) %copy-start) | copy-done | bytes 589848
  1.7 0.0 copy-start.1
  1.7 0.9 %copy-done.1 = bf16[256,384]{1,0:T(8,128)(2,1)S(1)} copy-done((bf16[256,384]{1,0:T(8,128)(2,1)S(1)}, bf16[256,384]{1,0:T(8,128)(2,1)}, u32[]{:S(2)}) %copy-start.1) | copy-done | bytes 196632
  2.6 0.0 copy-start.2
  2.6 0.7 %copy-done.2 = f32[2048]{0:T(1024)S(1)} copy-done((f32[2048]{0:T(1024)S(1)}, f32[2048]{0:T(1024)}, u32[]{:S(2)}) %copy-start.2) | copy-done | bytes 8216
  3.3 0.0 copy-start.3
  3.3 0.7 %copy-done.3 = s32[4]{0:T(128)S(1)} copy-done((s32[4]{0:T(128)S(1)}, s32[4]{0:T(128)}, u32[]{:S(2)}) %copy-start.3) | copy-done | bytes 40
  4.0 51.3 %shard_map.59 = (bf16[256,384]{1,0:T(8,128)(2,1)S(1)}, bf16[2,6,192,128]{3,2,1,0:T(8,128)(2,1)S(1)}) custom-call(bf16[256,384]{1,0:T(8,128)(2,1)S(1)} %copy-done.1, bf16[384,768]{1,0:T(8,128)(2,1)S(1)} %copy-done, f32[16,128]{1,0:T(8,128)S(1)} %bitcast.1, s32[4]{0:T(128)S(1)} %copy-done.3), custom_call_target="tpu_custom_call" | custom-call | tf_op jit(solution)/shard_map/pallas_call | solution.py:451
  55.3 1.1 %shard_map.60 = (bf16[256,384]{1,0:T(8,128)(2,1)}, f32[384,768]{1,0:T(8,128)}) custom-call(bf16[256,384]{1,0:T(8,128)(2,1)S(1)} %get-tuple-element.4.embed_ref, bf16[2,6,192,128]{3,2,1,0:T(8,128)(2,1)S(1)} %get-tuple-element.5.head_ref), custom_call_target="tpu_custom_call" | custom-call | tf_op jit(solution)/shard_map/pallas_call | solution.py:494
Async XLA Ops:
  0.6 1.1 %copy-start = (bf16[384,768]{1,0:T(8,128)(2,1)S(1)}, bf16[384,768]{1,0:T(8,128)(2,1)}, u32[]{:S(2)}) copy-start(bf16[384,768]{1,0:T(8,128)(2,1)} %head_ref.1) | copy-start | bytes 1769476
  1.7 0.9 %copy-start.1 = (bf16[256,384]{1,0:T(8,128)(2,1)S(1)}, bf16[256,384]{1,0:T(8,128)(2,1)}, u32[]{:S(2)}) copy-start(bf16[256,384]{1,0:T(8,128)(2,1)} %emb_ref.1) | copy-start | bytes 589828
  2.6 0.7 %copy-start.2 = (f32[2048]{0:T(1024)S(1)}, f32[2048]{0:T(1024)}, u32[]{:S(2)}) copy-start(f32[2048]{0:T(1024)} %param.6) | copy-start | bytes 24580
  3.3 0.7 %copy-start.3 = (s32[4]{0:T(128)S(1)}, s32[4]{0:T(128)}, u32[]{:S(2)}) copy-start(s32[4]{0:T(128)} %counts_ref.1) | copy-start | bytes 52

commit v3 on v2

--- a/solution.py
+++ b/solution.py
@@ -10,6 +10,7 @@
 EPSILON = 1e-06
 PARTS = 6
 CHUNKS = 2
+VMEM_BYTES = 60 * 1024 * 1024
 MESH_ID = pl.DeviceIdType.MESH
 
 
@@ -17,10 +18,12 @@
     sizes,
     emb_ref,
     head_ref,
+    gp_hbm,
+    counts_hbm,
+    embed_out,
+    head_out,
     gp_ref,
     counts_ref,
-    embed_out,
-    head_out,
     e_all,
     w_all,
     f_own,
@@ -113,7 +116,12 @@
 
     own_emb = pltpu.make_async_copy(emb_ref, e_all.at[z, c, x], in_sem.at[0])
     own_emb.start()
-    own_head = []
+    own_head = [
+        pltpu.make_async_copy(gp_hbm, gp_ref, in_sem.at[1]),
+        pltpu.make_async_copy(counts_hbm, counts_ref, in_sem.at[2]),
+    ]
+    for copy in own_head:
+        copy.start()
     for cc in range(nc):
         for gg in range(ng):
             start = (cc * ng + gg) * quarter
@@ -121,7 +129,7 @@
                 pltpu.make_async_copy(
                     head_ref.at[pl.ds(start, quarter)],
                     w_all.at[x, cc, gg],
-                    in_sem.at[1 + cc * ng + gg],
+                    in_sem.at[3 + cc * ng + gg],
                 )
             )
             own_head[-1].start()
@@ -445,18 +453,19 @@
         raise ValueError("head rows")
     gp_rows = gp_weights.reshape(-1, 128)
     vmem = pl.BlockSpec(memory_space=pltpu.VMEM)
-    hbm = pl.BlockSpec(memory_space=pl.ANY)
+    hbm = pl.BlockSpec(memory_space=pltpu.HBM)
     dma = pltpu.SemaphoreType.DMA
-    held = 2 * (nz * nc * nx * rows * cols + nx * cols * feats)
     embed_grad, head_sum = pl.pallas_call(
         functools.partial(kernel, (nz, nx, nc, ng)),
         out_shape=(
             jax.ShapeDtypeStruct((rows, cols), jnp.bfloat16),
             jax.ShapeDtypeStruct((nc, PARTS, half, width), jnp.bfloat16),
         ),
-        in_specs=[hbm, hbm, vmem, pl.BlockSpec(memory_space=pltpu.SMEM)],
+        in_specs=[hbm, hbm, hbm, hbm],
         out_specs=(vmem, vmem),
         scratch_shapes=[
+            pltpu.VMEM(gp_rows.shape, jnp.float32),
+            pltpu.SMEM(counts.shape, jnp.int32),
             pltpu.VMEM((nz, nc, nx, rows, cols), jnp.bfloat16),
             pltpu.VMEM((nx, nc, ng, half // ng, feats), jnp.bfloat16),
             pltpu.VMEM((rows, feats), jnp.bfloat16),
@@ -478,7 +487,7 @@
             dma((nx - 1, max(ng - 1, 1))),
             dma((nx, ng)),
             dma((nx, ng)),
-            dma((1 + nc * ng,)),
+            dma((3 + nc * ng,)),
             dma((PARTS,)),
             dma((PARTS,)),
             dma((PARTS,)),
@@ -488,7 +497,7 @@
             dma((nc, PARTS)),
         ],
         compiler_params=pltpu.CompilerParams(
-            collective_id=0, has_side_effects=True, vmem_limit_bytes=held + 20 * 1024 * 1024
+            collective_id=0, has_side_effects=True, vmem_limit_bytes=VMEM_BYTES
         ),
     )(embeddings, head_weight, gp_rows, counts)
     return pl.pallas_call(

time: 56.7 us -> 54.7 us (0.965)
  local copies, waits for them, and re-layouts: 3.33 us -> 1.98 us
  Pallas kernels: 52.5 us -> 51.9 us
    unnamed x8 -> x4, local copies, waits for them, and re-layouts: 3.33 us -> 1.98 us
where the time goes in v3:
time: 54.7 us; the launch traced here: 54.5 us
  Pallas kernels  51.9 us (95%)
  local copies, waits for them, and re-layouts  1.98 us (4%)
  between operations  0.65 us (1%)
    pallas_call x1, Pallas kernels, body(): pl.pallas_call(functools.partial(kernel, (nz, nx, nc, ng)), out_shape=(ja...  50.8 us
    unnamed x4, local copies, waits for them, and re-layouts  1.98 us
    pallas_call x1, Pallas kernels, body(): pl.pallas_call(finish, out_shape=(jax.ShapeDtypeStruct((rows, cols), jnp....  1.14 us

profile of v3, /device:TPU:1, one launch (start us, length us, event | category | flops | bytes accessed | tf_op | source)
XLA Modules:
  0.0 54.5 jit_solution(444711006790967606)
XLA Ops:
  0.6 50.8 %shard_map.59 = (bf16[256,384]{1,0:T(8,128)(2,1)}, bf16[2,6,192,128]{3,2,1,0:T(8,128)(2,1)}) custom-call(bf16[256,384]{1,0:T(8,128)(2,1)} %emb_ref.1, bf16[384,768]{1,0:T(8,128)(2,1)} %head_ref.1, f32[16,128]{1,0:T(8,128)} %bitcast.1, s32[4]{0:T(128)} %counts_hbm.1), custom_call_target="tpu_custom_call" | custom-call | tf_op jit(solution)/shard_map/pallas_call | solution.py:458
  51.4 0.0 copy-start
  51.4 1.1 %copy-done = bf16[2,6,192,128]{3,2,1,0:T(8,128)(2,1)S(1)} copy-done((bf16[2,6,192,128]{3,2,1,0:T(8,128)(2,1)S(1)}, bf16[2,6,192,128]{3,2,1,0:T(8,128)(2,1)}, u32[]{:S(2)}) %copy-start) | copy-done | bytes 589848
  52.5 0.0 copy-start.1
  52.5 0.9 %copy-done.1 = bf16[256,384]{1,0:T(8,128)(2,1)S(1)} copy-done((bf16[256,384]{1,0:T(8,128)(2,1)S(1)}, bf16[256,384]{1,0:T(8,128)(2,1)}, u32[]{:S(2)}) %copy-start.1) | copy-done | bytes 196632
  53.4 1.1 %shard_map.60 = (bf16[256,384]{1,0:T(8,128)(2,1)}, f32[384,768]{1,0:T(8,128)}) custom-call(bf16[256,384]{1,0:T(8,128)(2,1)S(1)} %copy-done.1, bf16[2,6,192,128]{3,2,1,0:T(8,128)(2,1)S(1)} %copy-done), custom_call_target="tpu_custom_call" | custom-call | tf_op jit(solution)/shard_map/pallas_call | solution.py:503
Async XLA Ops:
  51.4 1.1 %copy-start = (bf16[2,6,192,128]{3,2,1,0:T(8,128)(2,1)S(1)}, bf16[2,6,192,128]{3,2,1,0:T(8,128)(2,1)}, u32[]{:S(2)}) copy-start(bf16[2,6,192,128]{3,2,1,0:T(8,128)(2,1)} %get-tuple-element.5.head_ref) | copy-start | bytes 1769476
  52.5 0.9 %copy-start.1 = (bf16[256,384]{1,0:T(8,128)(2,1)S(1)}, bf16[256,384]{1,0:T(8,128)(2,1)}, u32[]{:S(2)}) copy-start(bf16[256,384]{1,0:T(8,128)(2,1)} %get-tuple-element.4.embed_ref) | copy-start | bytes 589828

commit v4 on v3

--- a/solution.py
+++ b/solution.py
@@ -508,7 +508,7 @@
         ),
         in_specs=[vmem, vmem],
         out_specs=(vmem, vmem),
-        compiler_params=pltpu.CompilerParams(vmem_limit_bytes=12 * 1024 * 1024),
+        compiler_params=pltpu.CompilerParams(vmem_limit_bytes=VMEM_BYTES),
     )(embed_grad, head_sum)
 
 

time: 54.7 us -> 53.8 us (0.984)
  local copies, waits for them, and re-layouts: 1.98 us -> 0 us
  Pallas kernels: 51.9 us -> 53.1 us
    unnamed x4 -> x0, local copies, waits for them, and re-layouts: 1.98 us -> none
    pallas_call x1, Pallas kernels: 1.14 us -> 2.28 us  [body(): pl.pallas_call(finish, out_shape=(jax.ShapeDtypeStruct((rows, cols), jnp....]
where the time goes in v4:
time: 53.8 us; the launch traced here: 53.7 us
  Pallas kernels  53.1 us (99%)
  between operations  0.64 us (1%)
    pallas_call x1, Pallas kernels, body(): pl.pallas_call(functools.partial(kernel, (nz, nx, nc, ng)), out_shape=(ja...  50.8 us
    pallas_call x1, Pallas kernels, body(): pl.pallas_call(finish, out_shape=(jax.ShapeDtypeStruct((rows, cols), jnp....  2.28 us

profile of v4, /device:TPU:1, one launch (start us, length us, event | category | flops | bytes accessed | tf_op | source)
XLA Modules:
  0.0 53.7 jit_solution(5940840254951185439)
XLA Ops:
  0.6 50.8 %shard_map.59 = (bf16[256,384]{1,0:T(8,128)(2,1)}, bf16[2,6,192,128]{3,2,1,0:T(8,128)(2,1)}) custom-call(bf16[256,384]{1,0:T(8,128)(2,1)} %emb_ref.1, bf16[384,768]{1,0:T(8,128)(2,1)} %head_ref.1, f32[16,128]{1,0:T(8,128)} %bitcast.1, s32[4]{0:T(128)} %counts_hbm.1), custom_call_target="tpu_custom_call" | custom-call | tf_op jit(solution)/shard_map/pallas_call | solution.py:458
  51.4 2.3 %shard_map.60 = (bf16[256,384]{1,0:T(8,128)(2,1)}, f32[384,768]{1,0:T(8,128)}) custom-call(bf16[256,384]{1,0:T(8,128)(2,1)} %get-tuple-element.4.embed_ref, bf16[2,6,192,128]{3,2,1,0:T(8,128)(2,1)} %get-tuple-element.5.head_ref), custom_call_target="tpu_custom_call" | custom-call | tf_op jit(solution)/shard_map/pallas_call | solution.py:503
